TPU v7x, 32 devices: a whole 2x2x4 slice. The times are simulated.
32 devices in a mesh: group: 2 (over x), dp: 16 (over z, y, core).
Axes of the slice: x: 2, y: 2, z: 4, core: 2. Of those that a mesh axis runs over, the one named last changes fastest.
Arguments:
- inputs: bfloat16 [4096, 8192], P(('group', 'dp')), parts along dimension 0, may hold values from -6 to 6
- pack_dest: int32 [4096], P(('group', 'dp')), parts along dimension 0, may hold values from 0 to 2047, as said below
- row_adapter: int32 [4096], P(('group', 'dp')), parts along dimension 0, may hold values from 0 to 7, as said below
- value_matrix: bfloat16 [8192, 1024], P('dp'), may hold values from -0.0625 to 0.0625
- down_master: float32 [16384, 128], P(('group', 'dp')), parts along dimension 0, may hold values from -0.0625 to 0.0625
- up_master: float32 [256, 1024], P(('group', 'dp')), parts along dimension 0, may hold values from -1.5 to 1.5
- down_m: float32 [16384, 128], P(('group', 'dp')), parts along dimension 0, may hold values from -0.24 to 0.24
- down_v: float32 [16384, 128], P(('group', 'dp')), parts along dimension 0, may hold values from 0.0005 to 0.005
- up_m: float32 [256, 1024], P(('group', 'dp')), parts along dimension 0, may hold values from -0.03 to 0.03
- up_v: float32 [256, 1024], P(('group', 'dp')), parts along dimension 0, may hold values from 1e-05 to 0.0001
- value_gradient: bfloat16 [4096, 1024], P(('group', 'dp')), parts along dimension 0, may hold values from -6 to 6
Outputs:
- values: bfloat16 [4096, 1024], P(('group', 'dp')), parts along dimension 0
- input_gradient: bfloat16 [4096, 8192], P(('group', 'dp')), parts along dimension 0
- new_down: float32 [16384, 128], P(('group', 'dp')), parts along dimension 0
- new_down_m: float32 [16384, 128], P(('group', 'dp')), parts along dimension 0
- new_down_v: float32 [16384, 128], P(('group', 'dp')), parts along dimension 0
- new_up: float32 [256, 1024], P(('group', 'dp')), parts along dimension 0
- new_up_m: float32 [256, 1024], P(('group', 'dp')), parts along dimension 0
- new_up_v: float32 [256, 1024], P(('group', 'dp')), parts along dimension 0
There are 2 independent parts, one for each index of `group`. A program takes and returns all parts, laid end to end along the dimension named above; an argument that names none is the same for every part. Nothing has to cross between parts.
Inputs may be any that keep to these rules, and one draw needn't show every extreme that they name: pack_dest is a permutation of the rows; the 128 rows of each device go to exactly 8 packed positions on each device, position d * 128 to (d + 1) * 128 - 1 being device d's. row_adapter is constant over runs of packed rows (sequences).
All inputs are finite; a program needn't handle non-finite values.
Results may differ from a plain program's by a relative error of at most 0.0061.
Values may be sent and summed in bfloat16 or wider, within the bound.
A program may use at most 128 MiB of HBM per device.

v0:
```python
import jax
import jax.numpy as jnp
from jax import lax
from jax.sharding import PartitionSpec as P

RANK = 16


adapter_scale = 2.0
beta_one = 0.9
beta_two = 0.999
learn_rate = 0.001
adam_eps = 1e-08
first_fix = 1.0 - 0.9**10
second_fix = 1.0 - 0.999**10


def adam_update(param, moment, second, gradient):
    moment_new = beta_one * moment + (1.0 - beta_one) * gradient
    second_new = beta_two * second + (1.0 - beta_two) * gradient * gradient
    param_new = param - learn_rate * (moment_new / first_fix) / (
        jnp.sqrt(second_new / second_fix) + adam_eps
    )
    return (param_new, moment_new, second_new)


def contract_trailing(left, right):
    return lax.dot_general(
        left, right, (((1,), (1,)), ((), ())), preferred_element_type=jnp.float32
    )


def contract_first(left, right):
    return lax.dot_general(
        left, right, (((0,), (0,)), ((), ())), preferred_element_type=jnp.float32
    )


def local(
    inputs,
    pack_dest,
    row_adapter,
    value_matrix,
    down_master,
    up_master,
    down_m,
    down_v,
    up_m,
    up_v,
    value_gradient,
):
    device_list = lax.axis_size("dp")
    token_row_block = inputs.shape[0]
    width = inputs.shape[1]
    per_peer = token_row_block // device_list
    target = pack_dest // token_row_block
    ordering = jnp.argsort(target, stable=True)
    outgoing = inputs[ordering].reshape(device_list, per_peer, width)
    slot_ids = (pack_dest % token_row_block)[ordering].reshape(device_list, per_peer)
    arrived, arrived_slots = (
        lax.all_to_all(outgoing, "dp", split_axis=0, concat_axis=0, tiled=True),
        lax.all_to_all(slot_ids, "dp", split_axis=0, concat_axis=0, tiled=True),
    )
    placing = jnp.argsort(arrived_slots.reshape(token_row_block))
    packed_rows = arrived.reshape(token_row_block, width)[placing]
    down_complete, up_complete = (
        lax.all_gather(down_master.astype(jnp.bfloat16), "dp", axis=0, tiled=True),
        lax.all_gather(up_master.astype(jnp.bfloat16), "dp", axis=0, tiled=True),
    )
    columns = down_complete.shape[1]
    owners = lax.iota(jnp.int32, columns) // RANK
    chosen = row_adapter[:, None] == owners[None, :]
    back_full = jnp.where(chosen, contract_trailing(value_gradient, up_complete), 0.0)
    backward_pass = back_full.astype(jnp.bfloat16)
    weight_full = lax.all_gather(value_matrix, "dp", axis=0, tiled=True)
    frozen_output = jnp.dot(packed_rows, weight_full, preferred_element_type=jnp.float32)
    frozen_backward = contract_trailing(value_gradient, weight_full)
    low_rank_term = jnp.where(
        chosen, jnp.dot(packed_rows, down_complete, preferred_element_type=jnp.float32), 0.0
    ).astype(jnp.bfloat16)
    values = (
        frozen_output
        + adapter_scale * jnp.dot(low_rank_term, up_complete, preferred_element_type=jnp.float32)
    ).astype(jnp.bfloat16)
    input_gradient = (
        frozen_backward + adapter_scale * contract_trailing(backward_pass, down_complete)
    ).astype(jnp.bfloat16)
    scale_factor = adapter_scale / (token_row_block * device_list)
    portion = packed_rows
    grad_down = lax.psum_scatter(
        contract_first(portion, backward_pass) * scale_factor, "dp", scatter_dimension=0, tiled=True
    )
    portion = low_rank_term
    grad_up = lax.psum_scatter(
        contract_first(portion, value_gradient) * scale_factor,
        "dp",
        scatter_dimension=0,
        tiled=True,
    )
    new_down, new_down_m, new_down_v = adam_update(down_master, down_m, down_v, grad_down)
    new_up, new_up_m, new_up_v = adam_update(up_master, up_m, up_v, grad_up)
    return (values, input_gradient, new_down, new_down_m, new_down_v, new_up, new_up_m, new_up_v)


def solution(mesh):
    in_specs = (
        P(("group", "dp"), None),
        P(("group", "dp")),
        P(("group", "dp")),
        P("dp", None),
        P(("group", "dp"), None),
        P(("group", "dp"), None),
        P(("group", "dp"), None),
        P(("group", "dp"), None),
        P(("group", "dp"), None),
        P(("group", "dp"), None),
        P(("group", "dp"), None),
    )
    out_specs = (
        P(("group", "dp"), None),
        P(("group", "dp"), None),
        P(("group", "dp"), None),
        P(("group", "dp"), None),
        P(("group", "dp"), None),
        P(("group", "dp"), None),
        P(("group", "dp"), None),
        P(("group", "dp"), None),
    )
    return jax.shard_map(local, mesh=mesh, in_specs=in_specs, out_specs=out_specs, check_vma=False)
```

profile of v0, /device:TPU:0, one launch (start us, length us, event | category | flops | bytes accessed | tf_op | source)
XLA Modules:
  0.0 441.0 jit_solution(14803981038335953398)
XLA Ops:
  7.2 0.8 and_select_fusion.1
  8.0 2.5 sort.34
  10.5 1.2 gather_fusion.1
  11.8 0.7 all_to_all.10
  12.5 7.4 %all-to-all-start.1 = ((s32[16,1,8]{2,1,0:T(1,128)}), s32[16,1,8]{2,1,0:T(1,128)S(1)}, u32[]{:S(2)}, u32[]{:S(2)}) async-start(s32[16,1,8]{2,1,0:T(1,128)} %bitcast.2), calls=%async_computation.1 | async-start | bytes 16384 | tf_op jit(solution)/shard_map/all_to_all | solution.py:62
  19.9 3.2 gather_fusion
  23.1 3.1 all-to-all-done.1
  26.2 4.6 %all-to-all-start = ((bf16[16,8,8192]{2,1,0:T(8,128)(2,1)}), bf16[16,8,8192]{2,1,0:T(8,128)(2,1)}, u32[]{:S(2)}, u32[]{:S(2)}) async-start(bf16[16,8,8192]{2,1,0:T(8,128)(2,1)} %bitcast.19), calls=%async_computation | async-start | bytes 4194304 | tf_op jit(solution)/shard_map/all_to_all | solution.py:61
  30.9 55.0 %all_gather.11 = bf16[128,1024]{1,0:T(8,128)(2,1)S(1)} all-gather(bf16[8,1024]{1,0:T(8,128)(2,1)S(1)} %convert_element_type.20), channel_id=1, replica_groups=mesh['group'=2,'dp'=16] {'dp'}, dimensions={0}, use_global_device_ids=true | all-gather | bytes 278528 | tf_op jit(solution)/shard_map/all_gather | solution.py:68
  85.9 0.2 fusion.5
  86.1 0.5 broadcast.88
  86.6 0.7 reduce.3
  87.3 0.1 reshape.46
  87.4 2.5 sort.35
  89.9 6.9 %gather_fusion.2 = bf16[128,8192]{1,0:T(8,128)(2,1)} fusion(bf16[128,8192]{1,0:T(8,128)(2,1)} %bitcast.1, s32[1024]{0:T(1024)S(1)} %pad_clamp_fusion), kind=kCustom, calls=%fused_computation.2 | custom fusion | bytes 4194816 | tf_op jit(solution)/shard_map/gather | solution.py:65
  96.9 4.3 convolution_multiply_fusion
  101.2 0.0 all-gather.5.cloned.1.call-start
  101.2 75.2 %reduce-scatter.3.cloned.1.call-done = f32[512,128]{1,0:T(8,128)} async-done(((f32[8192,128]{1,0:T(8,128)}), f32[512,128]{1,0:T(8,128)}) %reduce-scatter.3.cloned.1.call-update) | async-done | bytes 262160 | tf_op jit(solution)/shard_map/reduce_scatter | solution.py:90
  176.5 2.0 divide_subtract_fusion
  178.5 0.0 reduce-scatter.5.cloned.1.call-start
  178.5 41.4 %all-gather.5.cloned.1.call-done = bf16[8192,128]{1,0:T(8,128)(2,1)} async-done(((bf16[512,128]{1,0:T(8,128)(2,1)}), bf16[8192,128]{1,0:T(8,128)(2,1)}) %all-gather.5.cloned.1.call-update) | async-done | bytes 2097168 | tf_op jit(solution)/shard_map/all_gather | solution.py:67
  220.0 2.9 fusion.4
  222.9 1.0 convolution_multiply_fusion.2
  224.0 0.2 all-gather.3.cloned.1.call-start
  224.2 0.3 all-gather.3.cloned.1.call-update
  224.6 54.2 %reduce-scatter.5.cloned.1.call-done = f32[8,1024]{1,0:T(8,128)} async-done(((f32[128,1024]{1,0:T(8,128)}), f32[8,1024]{1,0:T(8,128)}) %reduce-scatter.5.cloned.1.call-update) | async-done | bytes 32784 | tf_op jit(solution)/shard_map/reduce_scatter | solution.py:94
  278.8 1.4 divide_subtract_fusion.1
  280.2 126.5 %all-gather.3.cloned.1.call-done = bf16[8192,1024]{1,0:T(8,128)(2,1)} async-done(((bf16[512,1024]{1,0:T(8,128)(2,1)}), bf16[8192,1024]{1,0:T(8,128)(2,1)}) %all-gather.3.cloned.1.call-update) | async-done | bytes 16777232 | tf_op jit(solution)/shard_map/all_gather | solution.py:75
  406.7 8.7 %fusion.10 = f32[128,1024]{1,0:T(8,128)S(1)} fusion(bf16[128,8192]{1,0:T(8,128)(2,1)} %gather_fusion.2, bf16[8192,1024]{1,0:T(8,128)(2,1)} %all-gather.3.cloned.1.call-done), kind=kOutput, calls=%fused_computation.36 | convolution fusion | flops 2147483648 | bytes 19398656 | tf_op jit(solution)/shard_map/dot_general | solution.py:76
  415.4 0.9 fusion.3
  416.3 13.3 %fusion.11 = f32[128,8192]{1,0:T(8,128)} fusion(bf16[128,1024]{1,0:T(8,128)(2,1)S(1)} %copy-done.1, bf16[8192,1024]{1,0:T(8,128)(2,1)} %all-gather.3.cloned.1.call-done), kind=kOutput, calls=%fused_computation.37 | convolution fusion | flops 2147483648 | bytes 21233664 | tf_op jit(solution)/shard_map/dot_general | solution.py:28
  429.6 4.9 %fusion.1 = bf16[128,8192]{1,0:T(8,128)(2,1)} fusion(f32[128,8192]{1,0:T(8,128)} %fusion.11, bf16[128,128]{1,0:T(8,128)(2,1)S(1)} %fusion.5, bf16[8192,128]{1,0:T(8,128)(2,1)} %all-gather.5.cloned.1.call-done), kind=kOutput, calls=%fused_computation.6 | convolution fusion | flops 271581184 | bytes 8421376 | tf_op jit(solution)/shard_map/dot_general | solution.py:28
  (31 shorter events, 0.2 us)
Async XLA Ops:
  7.2 12.7 %copy-start = (bf16[128,8192]{1,0:T(8,128)(2,1)S(1)}, bf16[128,8192]{1,0:T(8,128)(2,1)}, u32[]{:S(2)}) copy-start(bf16[128,8192]{1,0:T(8,128)(2,1)} %param.11) | copy-start | bytes 6291460
  12.5 13.7 %all-to-all-start.1 = ((s32[16,1,8]{2,1,0:T(1,128)}), s32[16,1,8]{2,1,0:T(1,128)S(1)}, u32[]{:S(2)}, u32[]{:S(2)}) async-start(s32[16,1,8]{2,1,0:T(1,128)} %bitcast.2), calls=%async_computation.1 | async-start | bytes 16384 | tf_op jit(solution)/shard_map/all_to_all | solution.py:62
  26.2 4.6 %copy-start.5 = (f32[8,1024]{1,0:T(8,128)S(1)}, f32[8,1024]{1,0:T(8,128)}, u32[]{:S(2)}) copy-start(f32[8,1024]{1,0:T(8,128)} %param.16) | copy-start | bytes 98308
  26.2 59.7 %copy-start.1 = (bf16[128,1024]{1,0:T(8,128)(2,1)S(1)}, bf16[128,1024]{1,0:T(8,128)(2,1)}, u32[]{:S(2)}) copy-start(bf16[128,1024]{1,0:T(8,128)(2,1)} %param.21) | copy-start | bytes 786436
  26.2 59.7 %copy-start.8 = (s32[128]{0:T(128)S(1)}, s32[128]{0:T(128)}, u32[]{:S(2)}) copy-start(s32[128]{0:T(128)} %param.13) | copy-start | bytes 1540
  26.2 63.7 %all-to-all-start = ((bf16[16,8,8192]{2,1,0:T(8,128)(2,1)}), bf16[16,8,8192]{2,1,0:T(8,128)(2,1)}, u32[]{:S(2)}, u32[]{:S(2)}) async-start(bf16[16,8,8192]{2,1,0:T(8,128)(2,1)} %bitcast.19), calls=%async_computation | async-start | bytes 4194304 | tf_op jit(solution)/shard_map/all_to_all | solution.py:61
  30.8 145.7 %reduce-scatter.3.cloned.1.call-start = ((), (), s32[]{:S(2)}) async-start(), calls=%async_computation.6 | async-start | bytes 4456448 | tf_op jit(solution)/shard_map/reduce_scatter | solution.py:90
  101.2 75.3 %copy-start.2 = (f32[512,128]{1,0:T(8,128)S(1)}, f32[512,128]{1,0:T(8,128)}, u32[]{:S(2)}) copy-start(f32[512,128]{1,0:T(8,128)} %param.15) | copy-start | bytes 786436
  101.2 75.3 %copy-start.3 = (f32[512,128]{1,0:T(8,128)S(1)}, f32[512,128]{1,0:T(8,128)}, u32[]{:S(2)}) copy-start(f32[512,128]{1,0:T(8,128)} %param.17) | copy-start | bytes 786436
  101.2 75.3 %copy-start.4 = (f32[512,128]{1,0:T(8,128)S(1)}, f32[512,128]{1,0:T(8,128)}, u32[]{:S(2)}) copy-start(f32[512,128]{1,0:T(8,128)} %param.18) | copy-start | bytes 786436
  101.2 118.8 %all-gather.5.cloned.1.call-start = ((), (), s32[]{:S(2)}) async-start(), calls=%async_computation.5 | async-start | bytes 2228224 | tf_op jit(solution)/shard_map/all_gather | solution.py:67
  178.5 100.3 %reduce-scatter.5.cloned.1.call-start = ((), (), s32[]{:S(2)}) async-start(), calls=%async_computation.7 | async-start | bytes 557056 | tf_op jit(solution)/shard_map/reduce_scatter | solution.py:94
  222.9 55.8 %copy-start.6 = (f32[8,1024]{1,0:T(8,128)S(1)}, f32[8,1024]{1,0:T(8,128)}, u32[]{:S(2)}) copy-start(f32[8,1024]{1,0:T(8,128)} %param.19) | copy-start | bytes 98308
  222.9 55.8 %copy-start.7 = (f32[8,1024]{1,0:T(8,128)S(1)}, f32[8,1024]{1,0:T(8,128)}, u32[]{:S(2)}) copy-start(f32[8,1024]{1,0:T(8,128)} %param.20) | copy-start | bytes 98308
  224.0 182.7 %all-gather.3.cloned.1.call-start = ((), (), s32[]{:S(2)}) async-start(), calls=%async_computation.4 | async-start | bytes 17825792 | tf_op jit(solution)/shard_map/all_gather | solution.py:75
Sparse Core Ops, SparseCore 0:
  101.3 75.1 reduce-scatter.2
  179.5 40.4 all-gather.4
  224.1 54.5 reduce-scatter.4
  280.8 125.8 all-gather.2
where the time goes:
time: 441 us
  waiting for transfers between devices  301 us (68%)
  blocking collectives  55 us (12%)
  matrix products  36.2 us (8%)
  between operations  13.9 us (3%)
  local copies, waits for them, and re-layouts  12.7 us (3%)
  starting transfers between devices  12.3 us (3%)
  other arithmetic  9.96 us (2%)
    all_gather x1, waiting for transfers between devices, local(): weight_full = lax.all_gather(value_matrix, 'dp', axis=0, tiled=True)  127 us
    reduce_scatter x1, waiting for transfers between devices, local(): lax.psum_scatter(contract_first(portion, backward_pass) * scale_factor, '...  75.2 us
    all_gather x1, blocking collectives, local(): lax.all_gather(up_master.astype(jnp.bfloat16), 'dp', axis=0, tiled=True)  55 us
    reduce_scatter x1, waiting for transfers between devices, local(): lax.psum_scatter(contract_first(portion, value_gradient) * scale_factor,...  54.2 us
    all_gather x1, waiting for transfers between devices, local(): lax.all_gather(down_master.astype(jnp.bfloat16), 'dp', axis=0, tiled=True)  41.4 us
    dot_general x3, matrix products, contract_trailing(): lax.dot_general(left, right, (((1,), (1,)), ((), ())), preferred_element_...  18.3 us
  transfers between devices with their start and end apart: 6, of which 5 were waited for; matrix products, arithmetic and copies ran while one was open for 2% of the time, Pallas kernels for 0%

commit v1 on v0

v1 whole, which is shorter than its diff:
```python
import functools

import jax
import jax.numpy as jnp
from jax import lax
from jax.experimental import pallas as pl
from jax.experimental.pallas import tpu as pltpu
from jax.sharding import PartitionSpec as P

RANK = 16
PAD = 16
MESH = pl.DeviceIdType.MESH

adapter_scale = 2.0
beta_one = 0.9
beta_two = 0.999
learn_rate = 0.001
adam_eps = 1e-08
first_fix = 1.0 - 0.9**10
second_fix = 1.0 - 0.999**10

bf16, f32, i32 = jnp.bfloat16, jnp.float32, jnp.int32


def adam_update(param, moment, second, gradient):
    moment_new = beta_one * moment + (1.0 - beta_one) * gradient
    second_new = beta_two * second + (1.0 - beta_two) * gradient * gradient
    param_new = param - learn_rate * (moment_new / first_fix) / (
        jnp.sqrt(second_new / second_fix) + adam_eps
    )
    return (param_new, moment_new, second_new)


def dot(left, right, lc=1, rc=0):
    return lax.dot_general(
        left, right, (((lc,), (rc,)), ((), ())), preferred_element_type=f32
    )


def iota(shape, dim):
    return lax.broadcasted_iota(i32, shape, dim)


def onehot(cond):
    return jnp.where(cond, 1.0, 0.0).astype(bf16)


def kernel(
    n,
    up_rows,
    x_ref,
    pd_col_ref,
    pd_row_ref,
    ra_col_ref,
    wd_ref,
    upad_ref,
    dv_ref,
    values_ref,
    ig_ref,
    gd_ref,
    gu_ref,
    wd_all,
    up_all,
    b_all,
    g_send,
    g_recv,
    v_send,
    v_recv,
    u_send,
    u_recv,
    acc,
    dvb,
    ring_send,
    ring_recv,
    sib_send,
    sib_recv,
    push_send,
    push_recv,
):
    tok = x_ref.shape[0]
    depth, wide = wd_ref.shape
    dv_width = dv_ref.shape[1]
    cols = wide - dv_width
    chips = n // 2
    half = depth // 2
    me = lax.axis_index("dp")
    core = lax.rem(me, 2)
    chip = me // 2
    zs = chips // 2

    def place_of(c):
        z, y = c // 2, lax.rem(c, 2)
        return jnp.where(y == 0, z, chips - 1 - z)

    def chip_at(p):
        p = lax.rem(p + chips, chips)
        return jnp.where(p < zs, 2 * p, 2 * (chips - 1 - p) + 1)

    place = place_of(chip)
    sibling = 2 * chip + 1 - core

    barrier = pltpu.get_barrier_semaphore()

    @pl.loop(1, n)
    def _(j):
        pl.semaphore_signal(
            barrier, inc=1, device_id={"dp": lax.rem(me + j, n)}, device_id_type=MESH
        )

    pl.semaphore_wait(barrier, n - 1)

    def push(phase, j, src, dst):
        return pltpu.make_async_remote_copy(
            src_ref=src,
            dst_ref=dst,
            send_sem=push_send.at[phase, j],
            recv_sem=push_recv.at[phase, j],
            device_id={"dp": lax.rem(me + j, n)},
            device_id_type=MESH,
        )

    def push_all(phase, src_of, dst):
        @pl.loop(1, n)
        def _(j):
            push(phase, j, src_of(lax.rem(me + j, n)), dst).start()

    def wait_all(phase, src_of, dst):
        @pl.loop(1, n)
        def _(j):
            push(phase, j, src_of(lax.rem(me + j, n)), dst).wait()

    last = chips // 2

    def part_of(idx, step, way):
        if step < last:
            return wd_all.at[idx]
        return wd_all.at[idx, pl.ds(way * half, half)]

    def source_place(step, way):
        return place - step if way == 0 else place + step

    def ring(step, way):
        target = place + 1 if way == 0 else place - 1
        origin = 2 * chip_at(source_place(step - 1, way)) + core
        return pltpu.make_async_remote_copy(
            src_ref=part_of(origin, step, way),
            dst_ref=part_of(origin, step, way),
            send_sem=ring_send.at[way, step],
            recv_sem=ring_recv.at[way, step],
            device_id={"dp": 2 * chip_at(target) + core},
            device_id_type=MESH,
        )

    def sib(step, way):
        origin = 2 * chip_at(source_place(step, way)) + core
        return pltpu.make_async_remote_copy(
            src_ref=part_of(origin, step, way),
            dst_ref=part_of(origin, step, way),
            send_sem=sib_send.at[way, step],
            recv_sem=sib_recv.at[way, step],
            device_id={"dp": sibling},
            device_id_type=MESH,
        )

    up_all[me] = upad_ref[...]
    push_all(0, lambda d: upad_ref, up_all.at[me])
    wd_all[me] = wd_ref[...]
    ring(1, 0).start()
    ring(1, 1).start()
    sib(0, 0).start()
    wait_all(0, lambda d: upad_ref, up_all.at[me])

    up_flat = up_all[...].reshape(n * PAD, dv_width)
    q = iota((cols, n * PAD), 1)
    r = iota((cols, n * PAD), 0)
    spread = onehot((q % PAD < up_rows) & ((q // PAD) * up_rows + q % PAD == r))
    up_full = dot(spread, up_flat).astype(bf16)
    owner = iota((tok, cols), 1) // RANK
    back = dot(dv_ref[...], up_full, 1, 1)
    back = jnp.where(ra_col_ref[...] == owner, back, 0.0).astype(bf16)
    b_all[me] = back
    push_all(1, lambda d: b_all.at[me], b_all.at[me])
    dvb[:, :dv_width] = dv_ref[...]
    dvb[:, dv_width:] = (back.astype(f32) * adapter_scale).astype(bf16)
    acc[...] = jnp.zeros_like(acc)

    def work(p, k):
        d = 2 * chip_at(p) + k
        where = pl.ds(pl.multiple_of(d * depth, depth), depth)
        block = wd_all[d]
        acc[...] += dot(x_ref[:, where], block)
        ig_ref[:, where] = dot(dvb[...], block, 1, 1).astype(bf16)

    def step_on(step):
        for way in (0, 1):
            ring(step, way).wait_recv()
            if step < last:
                ring(step + 1, way).start()
            sib(step, way).start()

    step_on(1)
    work(place, core)

    wait_all(1, lambda d: b_all.at[me], b_all.at[me])
    pd_col = pd_col_ref[...]

    def pick(d, carry):
        rows, adapter = carry
        hit = pd_col == d * tok + iota((tok, tok), 1)
        rows = rows + dot(onehot(hit), b_all[d])
        ad = up_all[d][up_rows : up_rows + 1, :tok].astype(f32)
        adapter = adapter + jnp.sum(jnp.where(hit, ad, 0.0), axis=1, keepdims=True)
        return rows, adapter

    home, adapter = lax.fori_loop(
        0, n, pick, (jnp.zeros((tok, cols), f32), jnp.zeros((tok, 1), f32))
    )
    home = home.astype(bf16)
    scale_factor = adapter_scale / (tok * n)

    @pl.loop(0, n)
    def _(d):
        where = pl.ds(pl.multiple_of(d * depth, depth), depth)
        g_send[d] = (dot(x_ref[:, where], home, 0, 0) * scale_factor).astype(bf16)

    push_all(2, lambda d: g_send.at[d], g_recv.at[me])
    g_recv[me] = g_send[me]

    sib(0, 0).wait_recv()
    work(place, 1 - core)
    for step in range(2, last + 1):
        step_on(step)
        for way in (0, 1):
            work(source_place(step - 1, way), core)
            sib(step - 1, way).wait_recv()
            work(source_place(step - 1, way), 1 - core)
    work(place + last, core)
    sib(last, 0).wait_recv()
    sib(last, 1).wait_recv()
    work(place + last, 1 - core)

    low = jnp.where(adapter == owner.astype(f32), acc[:, dv_width:], 0.0).astype(bf16)
    val = (acc[:, :dv_width] + adapter_scale * dot(low, up_full)).astype(bf16)
    tr = pd_row_ref[...] // tok
    same = (pd_col // tok == tr) & (iota((tok, tok), 0) < iota((tok, tok), 1))
    turn = jnp.sum(jnp.where(same, 1.0, 0.0), axis=0, keepdims=True).astype(i32)
    order = onehot(tr * PAD + turn == iota((n * PAD, tok), 0))
    slot = jnp.broadcast_to((pd_col % tok + 1).astype(f32), (tok, tok)).astype(bf16)
    for part, lo, hi in (
        (val, 0, dv_width),
        (low, dv_width, wide),
        (slot, wide, wide + tok),
    ):
        v_send[:, :, lo:hi] = dot(order, part).astype(bf16).reshape(n, PAD, hi - lo)
    push_all(3, lambda d: v_send.at[d], v_recv.at[me])
    v_recv[me] = v_send[me]

    wait_all(2, lambda d: g_send.at[d], g_recv.at[me])
    gd_ref[...] = lax.fori_loop(
        0, n, lambda d, s: s + g_recv[d].astype(f32), jnp.zeros(gd_ref.shape, f32)
    )

    wait_all(3, lambda d: v_send.at[d], v_recv.at[me])
    got = v_recv[...].reshape(n * PAD, wide + tok)
    put = onehot(got[:, wide:].astype(f32) == (iota((n * PAD, tok), 1) + 1).astype(f32))
    packed = dot(put, got[:, :wide], 0, 0).astype(bf16)
    values_ref[...] = packed[:, :dv_width]

    low_wide = dot(packed[:, dv_width:], spread).astype(bf16)
    grad_up = dot(low_wide, dv_ref[...], 0, 0) * scale_factor
    u_send[...] = grad_up.astype(bf16).reshape(n, PAD, dv_width)
    push_all(4, lambda d: u_send.at[d], u_recv.at[me])
    u_recv[me] = u_send[me]

    for way in (0, 1):
        for step in range(1, last + 1):
            ring(step, way).wait_send()
            sib(step, way).wait_send()
    sib(0, 0).wait_send()

    wait_all(4, lambda d: u_send.at[d], u_recv.at[me])
    gu_ref[...] = lax.fori_loop(
        0, n, lambda d, s: s + u_recv[d].astype(f32), jnp.zeros(gu_ref.shape, f32)
    )


def local(
    n,
    inputs,
    pack_dest,
    row_adapter,
    value_matrix,
    down_master,
    up_master,
    down_m,
    down_v,
    up_m,
    up_v,
    value_gradient,
):
    tok, width = inputs.shape
    depth, dv_width = value_matrix.shape
    cols = down_master.shape[1]
    up_rows = up_master.shape[0]
    wide = dv_width + cols
    wd = jnp.concatenate([value_matrix, down_master.astype(bf16)], axis=1)
    upad = jnp.zeros((PAD, dv_width), bf16)
    upad = upad.at[:up_rows].set(up_master.astype(bf16))
    upad = upad.at[up_rows, :tok].set(row_adapter.astype(bf16))
    steps = n // 4 + 1
    vmem = pl.BlockSpec(memory_space=pltpu.VMEM)
    values, input_gradient, grad_down, grad_up = pl.pallas_call(
        functools.partial(kernel, n, up_rows),
        out_shape=(
            jax.ShapeDtypeStruct((tok, dv_width), bf16),
            jax.ShapeDtypeStruct((tok, width), bf16),
            jax.ShapeDtypeStruct((depth, cols), f32),
            jax.ShapeDtypeStruct((PAD, dv_width), f32),
        ),
        in_specs=[vmem] * 7,
        out_specs=[vmem] * 4,
        scratch_shapes=[
            pltpu.VMEM((n, depth, wide), bf16),
            pltpu.VMEM((n, PAD, dv_width), bf16),
            pltpu.VMEM((n, tok, cols), bf16),
            pltpu.VMEM((n, depth, cols), bf16),
            pltpu.VMEM((n, depth, cols), bf16),
            pltpu.VMEM((n, PAD, wide + tok), bf16),
            pltpu.VMEM((n, PAD, wide + tok), bf16),
            pltpu.VMEM((n, PAD, dv_width), bf16),
            pltpu.VMEM((n, PAD, dv_width), bf16),
            pltpu.VMEM((tok, wide), f32),
            pltpu.VMEM((tok, wide), bf16),
            pltpu.SemaphoreType.DMA((2, steps)),
            pltpu.SemaphoreType.DMA((2, steps)),
            pltpu.SemaphoreType.DMA((2, steps)),
            pltpu.SemaphoreType.DMA((2, steps)),
            pltpu.SemaphoreType.DMA((5, n)),
            pltpu.SemaphoreType.DMA((5, n)),
        ],
        compiler_params=pltpu.CompilerParams(
            collective_id=0, has_side_effects=True, vmem_limit_bytes=56 * 2**20
        ),
        cost_estimate=pl.CostEstimate(
            flops=6 * tok * width * wide,
            bytes_accessed=2 * (2 * tok * width + width * wide),
            transcendentals=0,
        ),
    )(
        inputs,
        pack_dest.reshape(tok, 1),
        pack_dest.reshape(1, tok),
        row_adapter.reshape(tok, 1),
        wd,
        upad,
        value_gradient,
    )
    new_down, new_down_m, new_down_v = adam_update(down_master, down_m, down_v, grad_down)
    new_up, new_up_m, new_up_v = adam_update(up_master, up_m, up_v, grad_up[:up_rows])
    return (values, input_gradient, new_down, new_down_m, new_down_v, new_up, new_up_m, new_up_v)


def solution(mesh):
    both = P(("group", "dp"), None)
    line = P(("group", "dp"))
    in_specs = (both, line, line, P("dp", None)) + (both,) * 7
    return jax.shard_map(
        functools.partial(local, mesh.shape["dp"]),
        mesh=mesh,
        in_specs=in_specs,
        out_specs=(both,) * 8,
        check_vma=False,
    )
```

time: 441 us -> 215 us (0.49)
  waiting for transfers between devices: 301 us -> 0 us
  Pallas kernels: 0 us -> 198 us
  blocking collectives: 55 us -> 0 us
  matrix products: 36.2 us -> 0 us
  between operations: 13.9 us -> 0.74 us
  starting transfers between devices: 12.3 us -> 0 us
  local copies, waits for them, and re-layouts: 12.7 us -> 6.6 us
    pallas_call x0 -> x1, Pallas kernels: none -> 198 us  [local(): pl.pallas_call(functools.partial(kernel, n, up_rows), out_shape=(jax.Shap...]
    all_gather x2 -> x0, waiting for transfers between devices: 168 us -> none  [the longest x1 127 us: local(): weight_full = lax.all_gather(value_matrix, 'dp', axis=0, tiled=True)]
    reduce_scatter x2 -> x0, waiting for transfers between devices: 129 us -> none  [the longest x1 75.2 us: local(): lax.psum_scatter(contract_first(portion, backward_pass) * scale_factor, '...]
    all_gather x1 -> x0, blocking collectives: 55 us -> none  [local(): lax.all_gather(up_master.astype(jnp.bfloat16), 'dp', axis=0, tiled=True)]
    dot_general x8 -> x0, matrix products: 36.2 us -> none  [the longest x3 18.3 us: contract_trailing(): lax.dot_general(left, right, (((1,), (1,)), ((), ())), preferred_element_...]
    all_to_all x2 -> x0, starting transfers between devices: 11.9 us -> none  [the longest x1 7.39 us: local(): lax.all_to_all(slot_ids, 'dp', split_axis=0, concat_axis=0, tiled=True)]
    gather x3 -> x0, local copies, waits for them, and re-layouts: 11.4 us -> none  [the longest x1 6.94 us: local(): packed_rows = arrived.reshape(token_row_block, width)[placing]]
    sort x2 -> x0, other arithmetic: 5.07 us -> none  [the longest x1 2.54 us: local(): ordering = jnp.argsort(target, stable=True)]
  transfers between devices with their start and end apart: 6 -> 0, of which waited for: 5 -> 0; matrix products, arithmetic and copies ran while one was open for 2% -> 0% of each run, Pallas kernels for 0% -> 0%
where the time goes in v1:
time: 215 us; the launch traced here: 212 us
  Pallas kernels  198 us (92%)
  other arithmetic  6.77 us (3%)
  local copies, waits for them, and re-layouts  6.6 us (3%)
    pallas_call x1, Pallas kernels, local(): pl.pallas_call(functools.partial(kernel, n, up_rows), out_shape=(jax.Shap...  198 us

profile of v1, /device:TPU:0, one launch (start us, length us, event | category | flops | bytes accessed | tf_op | source)
XLA Modules:
  0.0 212.0 jit_solution(6180366494450054578)
XLA Ops:
  0.6 0.0 copy-start.8
  0.6 0.0 copy-start.4
  0.7 1.4 copy.19.pd_col_ref
  2.1 1.4 copy.20.ra_col_ref
  3.4 1.0 convert_element_type.9
  4.4 2.3 %pad_maximum_fusion.wd_ref = bf16[512,1152]{1,0:T(8,128)(2,1)} fusion(bf16[512,128]{1,0:T(8,128)(2,1)S(1)} %convert_element_type.9, bf16[512,1024]{1,0:T(8,128)(2,1)} %param.18), kind=kLoop, calls=%fused_computation | loop fusion | flops 2359296 | bytes 2359296 | tf_op jit(solution)/shard_map/concatenate | solution.py:306
  6.7 0.0 copy-done.4
  6.8 0.0 copy-done.8
  6.8 0.2 scatter.9.upad_ref
  7.0 0.0 copy-start.7
  7.0 0.6 copy-done.7
  7.6 0.0 copy-start.1
  7.6 0.0 copy-start.2
  7.6 0.0 copy-start.3
  7.6 0.0 copy-start.5
  7.6 0.0 copy-start.6
  7.6 197.9 %shard_map.170 = (bf16[128,1024]{1,0:T(8,128)(2,1)}, bf16[128,8192]{1,0:T(8,128)(2,1)}, f32[512,128]{1,0:T(8,128)}, f32[16,1024]{1,0:T(8,128)}) custom-call(bf16[128,8192]{1,0:T(8,128)(2,1)} %x_ref.1, s32[128,1]{1,0:T(8,128)} %copy.19.pd_col_ref, s32[1,128]{1,0:T(1,128)} %bitcast.7, s32[128,1]{1,0:T(8,128)} %copy.20.ra_col_ref, ...), custom_call_target="tpu_custom_call" | custom-call | flops 7247757312 | bytes 23068672 | tf_op jit(solution)/shard_map/pallas_call | solution.py:312
  205.5 0.0 copy-start
  205.5 0.0 copy-done.1
  205.5 0.0 copy-done.2
  205.5 0.0 copy-done.3
  205.6 2.1 divide_subtract_fusion
  207.6 0.0 copy-done.5
  207.6 0.0 copy-done.6
  207.6 1.4 divide_subtract_fusion.1
  209.0 1.7 copy.24
  210.7 0.0 copy-done
  210.7 1.3 copy.25
  (3 shorter events, 0.0 us)
Async XLA Ops:
  0.6 6.1 %copy-start.8 = (s32[128]{0:T(128)S(1)}, s32[128]{0:T(128)}, u32[]{:S(2)}) copy-start(s32[128]{0:T(128)} %param.17) | copy-start | bytes 1540
  0.6 6.1 %copy-start.4 = (f32[8,1024]{1,0:T(8,128)S(1)}, f32[8,1024]{1,0:T(8,128)}, u32[]{:S(2)}) copy-start(f32[8,1024]{1,0:T(8,128)} %param.20) | copy-start | bytes 98308
  7.0 0.6 copy-start.7
  7.6 197.9 %copy-start.1 = (f32[512,128]{1,0:T(8,128)S(1)}, f32[512,128]{1,0:T(8,128)}, u32[]{:S(2)}) copy-start(f32[512,128]{1,0:T(8,128)} %param.19) | copy-start | bytes 786436
  7.6 198.0 %copy-start.2 = (f32[512,128]{1,0:T(8,128)S(1)}, f32[512,128]{1,0:T(8,128)}, u32[]{:S(2)}) copy-start(f32[512,128]{1,0:T(8,128)} %param.21) | copy-start | bytes 786436
  7.6 198.0 %copy-start.3 = (f32[512,128]{1,0:T(8,128)S(1)}, f32[512,128]{1,0:T(8,128)}, u32[]{:S(2)}) copy-start(f32[512,128]{1,0:T(8,128)} %param.22) | copy-start | bytes 786436
  7.6 200.0 %copy-start.5 = (f32[8,1024]{1,0:T(8,128)S(1)}, f32[8,1024]{1,0:T(8,128)}, u32[]{:S(2)}) copy-start(f32[8,1024]{1,0:T(8,128)} %param.23) | copy-start | bytes 98308
  7.6 200.0 %copy-start.6 = (f32[8,1024]{1,0:T(8,128)S(1)}, f32[8,1024]{1,0:T(8,128)}, u32[]{:S(2)}) copy-start(f32[8,1024]{1,0:T(8,128)} %param.24) | copy-start | bytes 98308
  205.5 5.2 %copy-start = (bf16[128,8192]{1,0:T(8,128)(2,1)S(1)}, bf16[128,8192]{1,0:T(8,128)(2,1)}, u32[]{:S(2)}) copy-start(bf16[128,8192]{1,0:T(8,128)(2,1)} %get-tuple-element.55) | copy-start | bytes 6291460

commit v2 on v1

--- a/solution.py
+++ b/solution.py
@@ -9,6 +9,7 @@
 
 RANK = 16
 PAD = 16
+SIDE = PAD // 2
 MESH = pl.DeviceIdType.MESH
 
 adapter_scale = 2.0
@@ -62,8 +63,10 @@
     wd_all,
     up_all,
     b_all,
-    g_send,
-    g_recv,
+    grad,
+    grad_core,
+    grad_y,
+    grad_z,
     v_send,
     v_recv,
     u_send,
@@ -76,6 +79,10 @@
     sib_recv,
     push_send,
     push_recv,
+    pair_send,
+    pair_recv,
+    z_send,
+    z_recv,
 ):
     tok = x_ref.shape[0]
     depth, wide = wd_ref.shape
@@ -87,6 +94,8 @@
     core = lax.rem(me, 2)
     chip = me // 2
     zs = chips // 2
+    my_z, my_y = chip // 2, lax.rem(chip, 2)
+    left = dv_width // 2
 
     def place_of(c):
         z, y = c // 2, lax.rem(c, 2)
@@ -170,15 +179,21 @@
     sib(0, 0).start()
     wait_all(0, lambda d: upad_ref, up_all.at[me])
 
-    up_flat = up_all[...].reshape(n * PAD, dv_width)
+    up_flat = up_all[...].reshape(n * PAD, left + tok)[:, :left]
     q = iota((cols, n * PAD), 1)
     r = iota((cols, n * PAD), 0)
-    spread = onehot((q % PAD < up_rows) & ((q // PAD) * up_rows + q % PAD == r))
-    up_full = dot(spread, up_flat).astype(bf16)
+
+    def spread_of(side):
+        row = q % PAD - side * SIDE
+        return onehot((row >= 0) & (row < up_rows) & ((q // PAD) * up_rows + row == r))
+
+    spread = (spread_of(0), spread_of(1))
+    up_full = jnp.concatenate([dot(m, up_flat).astype(bf16) for m in spread], axis=1)
     owner = iota((tok, cols), 1) // RANK
     back = dot(dv_ref[...], up_full, 1, 1)
     back = jnp.where(ra_col_ref[...] == owner, back, 0.0).astype(bf16)
-    b_all[me] = back
+    fold = onehot(iota((RANK, cols), 1) % RANK == iota((RANK, cols), 0))
+    b_all[me] = dot(fold, back, 1, 1).astype(bf16)
     push_all(1, lambda d: b_all.at[me], b_all.at[me])
     dvb[:, :dv_width] = dv_ref[...]
     dvb[:, dv_width:] = (back.astype(f32) * adapter_scale).astype(bf16)
@@ -207,29 +222,85 @@
     def pick(d, carry):
         rows, adapter = carry
         hit = pd_col == d * tok + iota((tok, tok), 1)
-        rows = rows + dot(onehot(hit), b_all[d])
-        ad = up_all[d][up_rows : up_rows + 1, :tok].astype(f32)
+        rows = rows + dot(onehot(hit), b_all[d], 1, 1)
+        ad = up_all[d][:1, left:].astype(f32)
         adapter = adapter + jnp.sum(jnp.where(hit, ad, 0.0), axis=1, keepdims=True)
         return rows, adapter
 
     home, adapter = lax.fori_loop(
-        0, n, pick, (jnp.zeros((tok, cols), f32), jnp.zeros((tok, 1), f32))
-    )
-    home = home.astype(bf16)
+        0, n, pick, (jnp.zeros((tok, RANK), f32), jnp.zeros((tok, 1), f32))
+    )
+    home = dot(home.astype(bf16), fold)
+    home = jnp.where(adapter == owner.astype(f32), home, 0.0).astype(bf16)
     scale_factor = adapter_scale / (tok * n)
 
     @pl.loop(0, n)
     def _(d):
         where = pl.ds(pl.multiple_of(d * depth, depth), depth)
-        g_send[d] = (dot(x_ref[:, where], home, 0, 0) * scale_factor).astype(bf16)
-
-    push_all(2, lambda d: g_send.at[d], g_recv.at[me])
-    g_recv[me] = g_send[me]
-
+        c = d // 2
+        grad[d % 2, c % 2, c // 2] = (
+            dot(x_ref[:, where], home, 0, 0) * scale_factor
+        ).astype(bf16)
+
+    def pair(stage, src, dst, device):
+        return pltpu.make_async_remote_copy(
+            src_ref=src,
+            dst_ref=dst,
+            send_sem=pair_send.at[stage],
+            recv_sem=pair_recv.at[stage],
+            device_id={"dp": device},
+            device_id_type=MESH,
+        )
+
+    over_core = pair(0, grad.at[1 - core], grad_core, sibling)
+    over_y = pair(
+        1, grad.at[core, 1 - my_y], grad_y, 2 * (2 * my_z + 1 - my_y) + core
+    )
+
+    def over_z(j):
+        z = lax.rem(my_z + j, zs)
+        return pltpu.make_async_remote_copy(
+            src_ref=grad.at[core, my_y, z],
+            dst_ref=grad_z.at[my_z],
+            send_sem=z_send.at[j],
+            recv_sem=z_recv.at[j],
+            device_id={"dp": 2 * (2 * z + my_y) + core},
+            device_id_type=MESH,
+        )
+
+    def start_y():
+        over_core.wait()
+
+        @pl.loop(0, 2 * zs)
+        def _(i):
+            y, z = i // zs, i % zs
+            total = grad[core, y, z].astype(f32) + grad_core[y, z].astype(f32)
+            grad[core, y, z] = total.astype(bf16)
+
+        over_y.start()
+
+    def start_z():
+        over_y.wait()
+
+        @pl.loop(0, zs)
+        def _(z):
+            total = grad[core, my_y, z].astype(f32) + grad_y[z].astype(f32)
+            grad[core, my_y, z] = total.astype(bf16)
+
+        @pl.loop(1, zs)
+        def _(j):
+            over_z(j).start()
+
+        grad_z[my_z] = grad[core, my_y, my_z]
+
+    over_core.start()
     sib(0, 0).wait_recv()
     work(place, 1 - core)
+    start_y()
     for step in range(2, last + 1):
         step_on(step)
+        if step == 2:
+            start_z()
         for way in (0, 1):
             work(source_place(step - 1, way), core)
             sib(step - 1, way).wait_recv()
@@ -244,32 +315,45 @@
     tr = pd_row_ref[...] // tok
     same = (pd_col // tok == tr) & (iota((tok, tok), 0) < iota((tok, tok), 1))
     turn = jnp.sum(jnp.where(same, 1.0, 0.0), axis=0, keepdims=True).astype(i32)
-    order = onehot(tr * PAD + turn == iota((n * PAD, tok), 0))
+    spot = tr * PAD + turn
+    line = iota((n * PAD, tok), 0)
+    order = (onehot(spot == line), onehot(spot + SIDE == line))
     slot = jnp.broadcast_to((pd_col % tok + 1).astype(f32), (tok, tok)).astype(bf16)
-    for part, lo, hi in (
-        (val, 0, dv_width),
-        (low, dv_width, wide),
-        (slot, wide, wide + tok),
+    for (first, second), lo, hi in (
+        ((val[:, :left], val[:, left:]), 0, left),
+        ((low, slot), left, left + tok),
     ):
-        v_send[:, :, lo:hi] = dot(order, part).astype(bf16).reshape(n, PAD, hi - lo)
+        block = dot(order[0], first) + dot(order[1], second)
+        v_send[:, :, lo:hi] = block.astype(bf16).reshape(n, PAD, hi - lo)
     push_all(3, lambda d: v_send.at[d], v_recv.at[me])
     v_recv[me] = v_send[me]
 
-    wait_all(2, lambda d: g_send.at[d], g_recv.at[me])
+    @pl.loop(1, zs)
+    def _(j):
+        over_z(j).wait()
+
     gd_ref[...] = lax.fori_loop(
-        0, n, lambda d, s: s + g_recv[d].astype(f32), jnp.zeros(gd_ref.shape, f32)
+        0, zs, lambda z, s: s + grad_z[z].astype(f32), jnp.zeros(gd_ref.shape, f32)
     )
 
     wait_all(3, lambda d: v_send.at[d], v_recv.at[me])
-    got = v_recv[...].reshape(n * PAD, wide + tok)
-    put = onehot(got[:, wide:].astype(f32) == (iota((n * PAD, tok), 1) + 1).astype(f32))
-    packed = dot(put, got[:, :wide], 0, 0).astype(bf16)
-    values_ref[...] = packed[:, :dv_width]
-
-    low_wide = dot(packed[:, dv_width:], spread).astype(bf16)
-    grad_up = dot(low_wide, dv_ref[...], 0, 0) * scale_factor
-    u_send[...] = grad_up.astype(bf16).reshape(n, PAD, dv_width)
-    push_all(4, lambda d: u_send.at[d], u_recv.at[me])
+    got = v_recv[...].reshape(n * PAD, left + tok)
+    tag = v_recv[:, :, left:].astype(f32)
+    tag_up = jnp.concatenate([tag[:, SIDE:], tag[:, :SIDE]], axis=1)
+    wanted = (iota((n * PAD, tok), 1) + 1).astype(f32)
+    upper = line % PAD < SIDE
+    put_up = onehot(upper & (tag_up.reshape(n * PAD, tok) == wanted))
+    put_down = onehot(jnp.logical_not(upper) & (tag.reshape(n * PAD, tok) == wanted))
+    packed = dot(put_up, got, 0, 0).astype(bf16)
+    values_ref[:, :left] = packed[:, :left]
+    values_ref[:, left:] = dot(put_down, got[:, :left], 0, 0).astype(bf16)
+
+    low_packed = packed[:, left:]
+    low_wide = [dot(low_packed, m).astype(bf16) for m in spread]
+    grad_up = dot(low_wide[0], dv_ref[:, :left], 0, 0)
+    grad_up = (grad_up + dot(low_wide[1], dv_ref[:, left:], 0, 0)) * scale_factor
+    u_send[...] = grad_up.astype(bf16).reshape(n, PAD, left)
+    push_all(2, lambda d: u_send.at[d], u_recv.at[me])
     u_recv[me] = u_send[me]
 
     for way in (0, 1):
@@ -278,7 +362,7 @@
             sib(step, way).wait_send()
     sib(0, 0).wait_send()
 
-    wait_all(4, lambda d: u_send.at[d], u_recv.at[me])
+    wait_all(2, lambda d: u_send.at[d], u_recv.at[me])
     gu_ref[...] = lax.fori_loop(
         0, n, lambda d, s: s + u_recv[d].astype(f32), jnp.zeros(gu_ref.shape, f32)
     )
@@ -304,9 +388,12 @@
     up_rows = up_master.shape[0]
     wide = dv_width + cols
     wd = jnp.concatenate([value_matrix, down_master.astype(bf16)], axis=1)
-    upad = jnp.zeros((PAD, dv_width), bf16)
-    upad = upad.at[:up_rows].set(up_master.astype(bf16))
-    upad = upad.at[up_rows, :tok].set(row_adapter.astype(bf16))
+    left = dv_width // 2
+    up_b = up_master.astype(bf16)
+    gap = ((0, SIDE - up_rows), (0, 0))
+    halves = [jnp.pad(up_b[:, :left], gap), jnp.pad(up_b[:, left:], gap)]
+    adapters = jnp.broadcast_to(row_adapter.astype(bf16)[None, :], (PAD, tok))
+    upad = jnp.concatenate([jnp.concatenate(halves, axis=0), adapters], axis=1)
     steps = n // 4 + 1
     vmem = pl.BlockSpec(memory_space=pltpu.VMEM)
     values, input_gradient, grad_down, grad_up = pl.pallas_call(
@@ -315,28 +402,34 @@
             jax.ShapeDtypeStruct((tok, dv_width), bf16),
             jax.ShapeDtypeStruct((tok, width), bf16),
             jax.ShapeDtypeStruct((depth, cols), f32),
-            jax.ShapeDtypeStruct((PAD, dv_width), f32),
+            jax.ShapeDtypeStruct((PAD, left), f32),
         ),
         in_specs=[vmem] * 7,
         out_specs=[vmem] * 4,
         scratch_shapes=[
             pltpu.VMEM((n, depth, wide), bf16),
-            pltpu.VMEM((n, PAD, dv_width), bf16),
-            pltpu.VMEM((n, tok, cols), bf16),
-            pltpu.VMEM((n, depth, cols), bf16),
-            pltpu.VMEM((n, depth, cols), bf16),
-            pltpu.VMEM((n, PAD, wide + tok), bf16),
-            pltpu.VMEM((n, PAD, wide + tok), bf16),
-            pltpu.VMEM((n, PAD, dv_width), bf16),
-            pltpu.VMEM((n, PAD, dv_width), bf16),
+            pltpu.VMEM((n, PAD, left + tok), bf16),
+            pltpu.VMEM((n, RANK, tok), bf16),
+            pltpu.VMEM((2, 2, n // 4, depth, cols), bf16),
+            pltpu.VMEM((2, n // 4, depth, cols), bf16),
+            pltpu.VMEM((n // 4, depth, cols), bf16),
+            pltpu.VMEM((n // 4, depth, cols), bf16),
+            pltpu.VMEM((n, PAD, left + tok), bf16),
+            pltpu.VMEM((n, PAD, left + tok), bf16),
+            pltpu.VMEM((n, PAD, left), bf16),
+            pltpu.VMEM((n, PAD, left), bf16),
             pltpu.VMEM((tok, wide), f32),
             pltpu.VMEM((tok, wide), bf16),
             pltpu.SemaphoreType.DMA((2, steps)),
             pltpu.SemaphoreType.DMA((2, steps)),
             pltpu.SemaphoreType.DMA((2, steps)),
             pltpu.SemaphoreType.DMA((2, steps)),
-            pltpu.SemaphoreType.DMA((5, n)),
-            pltpu.SemaphoreType.DMA((5, n)),
+            pltpu.SemaphoreType.DMA((4, n)),
+            pltpu.SemaphoreType.DMA((4, n)),
+            pltpu.SemaphoreType.DMA((2,)),
+            pltpu.SemaphoreType.DMA((2,)),
+            pltpu.SemaphoreType.DMA((n // 4,)),
+            pltpu.SemaphoreType.DMA((n // 4,)),
         ],
         compiler_params=pltpu.CompilerParams(
             collective_id=0, has_side_effects=True, vmem_limit_bytes=56 * 2**20
@@ -355,8 +448,11 @@
         upad,
         value_gradient,
     )
+    grad_up = jnp.concatenate(
+        [grad_up[:up_rows], grad_up[SIDE : SIDE + up_rows]], axis=1
+    )
     new_down, new_down_m, new_down_v = adam_update(down_master, down_m, down_v, grad_down)
-    new_up, new_up_m, new_up_v = adam_update(up_master, up_m, up_v, grad_up[:up_rows])
+    new_up, new_up_m, new_up_v = adam_update(up_master, up_m, up_v, grad_up)
     return (values, input_gradient, new_down, new_down_m, new_down_v, new_up, new_up_m, new_up_v)
 
 

time: 215 us -> 154 us (0.72); the launches traced: 212 us -> 154 us
  Pallas kernels: 198 us -> 140 us
    pallas_call x1, Pallas kernels: 198 us -> 140 us  [local(): pl.pallas_call(functools.partial(kernel, n, up_rows), out_shape=(jax.Shap...]
where the time goes in v2:
time: 154 us
  Pallas kernels  140 us (91%)
  other arithmetic  6.63 us (4%)
  local copies, waits for them, and re-layouts  6.56 us (4%)
    pallas_call x1, Pallas kernels, local(): pl.pallas_call(functools.partial(kernel, n, up_rows), out_shape=(jax.Shap...  140 us

profile of v2, /device:TPU:0, one launch (start us, length us, event | category | flops | bytes accessed | tf_op | source)
XLA Modules:
  0.0 153.9 jit_solution(15375439680228040879)
XLA Ops:
  0.6 0.0 copy-start.7
  0.6 0.0 copy-start.4
  0.7 1.4 copy.19.pd_col_ref
  2.1 1.4 copy.20.ra_col_ref
  3.4 1.0 convert_element_type.9
  4.4 2.3 %pad_maximum_fusion.wd_ref = bf16[512,1152]{1,0:T(8,128)(2,1)} fusion(bf16[512,128]{1,0:T(8,128)(2,1)S(1)} %convert_element_type.9, bf16[512,1024]{1,0:T(8,128)(2,1)} %param.14), kind=kLoop, calls=%fused_computation | loop fusion | flops 2359296 | bytes 2359296 | tf_op jit(solution)/shard_map/concatenate | solution.py:390
  6.7 0.0 copy-done.4
  6.8 0.0 copy-done.7
  6.8 0.6 maximum_maximum_fusion.upad_ref
  7.4 0.0 copy-start.1
  7.4 0.0 copy-start.2
  7.4 0.0 copy-start.3
  7.4 0.0 copy-start.5
  7.4 0.0 copy-start.6
  7.4 140.0 %shard_map.170 = (bf16[128,1024]{1,0:T(8,128)(2,1)}, bf16[128,8192]{1,0:T(8,128)(2,1)}, f32[512,128]{1,0:T(8,128)}, f32[16,512]{1,0:T(8,128)}) custom-call(bf16[128,8192]{1,0:T(8,128)(2,1)} %x_ref.1, s32[128,1]{1,0:T(8,128)} %copy.19.pd_col_ref, s32[1,128]{1,0:T(1,128)} %bitcast.5, s32[128,1]{1,0:T(8,128)} %copy.20.ra_col_ref, ...), custom_call_target="tpu_custom_call" | custom-call | flops 7247757312 | bytes 23068672 | tf_op jit(solution)/shard_map/pallas_call | solution.py:399
  147.5 0.0 copy-start
  147.5 0.0 copy-done.1
  147.5 0.0 copy-done.2
  147.5 0.0 copy-done.3
  147.5 2.1 %divide_subtract_fusion = (f32[512,128]{1,0:T(8,128)}, f32[512,128]{1,0:T(8,128)}, f32[512,128]{1,0:T(8,128)}) fusion(f32[512,128]{1,0:T(8,128)S(1)} %copy-done.1, f32[512,128]{1,0:T(8,128)} %get-tuple-element.14, f32[512,128]{1,0:T(8,128)S(1)} %copy-done.2, f32[512,128]{1,0:T(8,128)S(1)} %copy-done.3), kind=kLoop, calls=%fused_computation.3 | loop fusion | flops 786432 | bytes 1835008 | tf_op jit(solution)/shard_map/sub | solution.py:29
  149.6 0.7 fusion.4
  150.3 0.0 copy-done.5
  150.3 0.0 copy-done.6
  150.3 0.7 divide_subtract_fusion.1
  150.9 1.7 %copy.23 = bf16[128,1024]{1,0:T(8,128)(2,1)} copy(bf16[128,1024]{1,0:T(8,128)(2,1)} %get-tuple-element.34) | data formatting | bytes 524288
  152.6 0.0 copy-done
  152.6 1.3 copy.24
  (4 shorter events, 0.0 us)
Async XLA Ops:
  0.6 6.1 %copy-start.7 = (s32[128]{0:T(128)S(1)}, s32[128]{0:T(128)}, u32[]{:S(2)}) copy-start(s32[128]{0:T(128)} %param.13) | copy-start | bytes 1540
  0.6 6.1 %copy-start.4 = (f32[8,1024]{1,0:T(8,128)S(1)}, f32[8,1024]{1,0:T(8,128)}, u32[]{:S(2)}) copy-start(f32[8,1024]{1,0:T(8,128)} %param.16) | copy-start | bytes 98308
  7.4 140.1 %copy-start.1 = (f32[512,128]{1,0:T(8,128)S(1)}, f32[512,128]{1,0:T(8,128)}, u32[]{:S(2)}) copy-start(f32[512,128]{1,0:T(8,128)} %param.15) | copy-start | bytes 786436
  7.4 140.1 %copy-start.2 = (f32[512,128]{1,0:T(8,128)S(1)}, f32[512,128]{1,0:T(8,128)}, u32[]{:S(2)}) copy-start(f32[512,128]{1,0:T(8,128)} %param.17) | copy-start | bytes 786436
  7.4 140.1 %copy-start.3 = (f32[512,128]{1,0:T(8,128)S(1)}, f32[512,128]{1,0:T(8,128)}, u32[]{:S(2)}) copy-start(f32[512,128]{1,0:T(8,128)} %param.18) | copy-start | bytes 786436
  7.4 142.9 %copy-start.5 = (f32[8,1024]{1,0:T(8,128)S(1)}, f32[8,1024]{1,0:T(8,128)}, u32[]{:S(2)}) copy-start(f32[8,1024]{1,0:T(8,128)} %param.19) | copy-start | bytes 98308
  7.4 142.9 %copy-start.6 = (f32[8,1024]{1,0:T(8,128)S(1)}, f32[8,1024]{1,0:T(8,128)}, u32[]{:S(2)}) copy-start(f32[8,1024]{1,0:T(8,128)} %param.20) | copy-start | bytes 98308
  147.5 5.2 %copy-start = (bf16[128,8192]{1,0:T(8,128)(2,1)S(1)}, bf16[128,8192]{1,0:T(8,128)(2,1)}, u32[]{:S(2)}) copy-start(bf16[128,8192]{1,0:T(8,128)(2,1)} %get-tuple-element.35) | copy-start | bytes 6291460

commit v3 on v2

--- a/solution.py
+++ b/solution.py
@@ -83,6 +83,10 @@
     pair_recv,
     z_send,
     z_recv,
+    low_send,
+    low_recv,
+    x_send,
+    x_recv,
 ):
     tok = x_ref.shape[0]
     depth, wide = wd_ref.shape
@@ -90,6 +94,9 @@
     cols = wide - dv_width
     chips = n // 2
     half = depth // 2
+    group = lax.axis_index("group")
+    mirror = group + 1 - 2 * lax.rem(group, 2)
+    part = lax.rem(group, 2)
     me = lax.axis_index("dp")
     core = lax.rem(me, 2)
     chip = me // 2
@@ -116,7 +123,8 @@
             barrier, inc=1, device_id={"dp": lax.rem(me + j, n)}, device_id_type=MESH
         )
 
-    pl.semaphore_wait(barrier, n - 1)
+    pl.semaphore_signal(barrier, inc=1, device_id={"group": mirror}, device_id_type=MESH)
+    pl.semaphore_wait(barrier, n)
 
     def push(phase, j, src, dst):
         return pltpu.make_async_remote_copy(
@@ -148,15 +156,46 @@
     def source_place(step, way):
         return place - step if way == 0 else place + step
 
+    def frozen(idx, step, way):
+        if step < 2:
+            return wd_all.at[idx]
+        if step < last:
+            rows = pl.ds(pl.multiple_of(part * half, half), half)
+        else:
+            start = part * half + way * (half // 2)
+            rows = pl.ds(pl.multiple_of(start, half // 2), half // 2)
+        return wd_all.at[idx, rows, pl.ds(0, dv_width)]
+
+    def to_next(ref, step, way, sends, recvs):
+        target = place + 1 if way == 0 else place - 1
+        return pltpu.make_async_remote_copy(
+            src_ref=ref,
+            dst_ref=ref,
+            send_sem=sends.at[way, step],
+            recv_sem=recvs.at[way, step],
+            device_id={"dp": 2 * chip_at(target) + core},
+            device_id_type=MESH,
+        )
+
     def ring(step, way):
-        target = place + 1 if way == 0 else place - 1
         origin = 2 * chip_at(source_place(step - 1, way)) + core
+        return to_next(frozen(origin, step, way), step, way, ring_send, ring_recv)
+
+    def ring_low(step, way):
+        origin = 2 * chip_at(source_place(step - 1, way)) + core
+        rows = pl.ds(0, depth) if step < last else pl.ds(way * half, half)
+        ref = wd_all.at[origin, rows, pl.ds(dv_width, cols)]
+        return to_next(ref, step, way, low_send, low_recv)
+
+    def across(step, way):
+        origin = 2 * chip_at(source_place(step, way)) + core
+        ref = frozen(origin, step, way)
         return pltpu.make_async_remote_copy(
-            src_ref=part_of(origin, step, way),
-            dst_ref=part_of(origin, step, way),
-            send_sem=ring_send.at[way, step],
-            recv_sem=ring_recv.at[way, step],
-            device_id={"dp": 2 * chip_at(target) + core},
+            src_ref=ref,
+            dst_ref=ref,
+            send_sem=x_send.at[way, step],
+            recv_sem=x_recv.at[way, step],
+            device_id={"group": mirror},
             device_id_type=MESH,
         )
 
@@ -211,6 +250,17 @@
             ring(step, way).wait_recv()
             if step < last:
                 ring(step + 1, way).start()
+            if step < 2:
+                sib(step, way).start()
+            else:
+                across(step, way).start()
+                ring_low(step, way).wait_recv()
+            if step < last:
+                ring_low(step + 1, way).start()
+
+    def complete(step, way):
+        if step >= 2:
+            across(step, way).wait_recv()
             sib(step, way).start()
 
     step_on(1)
@@ -302,9 +352,15 @@
         if step == 2:
             start_z()
         for way in (0, 1):
+            complete(step - 1, way)
+        for way in (0, 1):
             work(source_place(step - 1, way), core)
             sib(step - 1, way).wait_recv()
             work(source_place(step - 1, way), 1 - core)
+    across(last, 0).wait_recv()
+    across(last, 1).wait_recv()
+    sib(last, 0).start()
+    sib(last, 1).start()
     work(place + last, core)
     sib(last, 0).wait_recv()
     sib(last, 1).wait_recv()
@@ -359,6 +415,9 @@
     for way in (0, 1):
         for step in range(1, last + 1):
             ring(step, way).wait_send()
+            if step >= 2:
+                ring_low(step, way).wait_send()
+                across(step, way).wait_send()
             sib(step, way).wait_send()
     sib(0, 0).wait_send()
 
@@ -430,6 +489,10 @@
             pltpu.SemaphoreType.DMA((2,)),
             pltpu.SemaphoreType.DMA((n // 4,)),
             pltpu.SemaphoreType.DMA((n // 4,)),
+            pltpu.SemaphoreType.DMA((2, steps)),
+            pltpu.SemaphoreType.DMA((2, steps)),
+            pltpu.SemaphoreType.DMA((2, steps)),
+            pltpu.SemaphoreType.DMA((2, steps)),
         ],
         compiler_params=pltpu.CompilerParams(
             collective_id=0, has_side_effects=True, vmem_limit_bytes=56 * 2**20

time: 154 us -> 148 us (0.961)
  Pallas kernels: 140 us -> 134 us
    pallas_call x1, Pallas kernels: 140 us -> 134 us  [local(): pl.pallas_call(functools.partial(kernel, n, up_rows), out_shape=(jax.Shap...]
where the time goes in v3:
time: 148 us
  Pallas kernels  134 us (91%)
  other arithmetic  6.63 us (4%)
  local copies, waits for them, and re-layouts  6.56 us (4%)
    pallas_call x1, Pallas kernels, local(): pl.pallas_call(functools.partial(kernel, n, up_rows), out_shape=(jax.Shap...  134 us
    unnamed x18, local copies, waits for them, and re-layouts  3.02 us

profile of v3, /device:TPU:0, one launch (start us, length us, event | category | flops | bytes accessed | tf_op | source)
XLA Modules:
  0.0 147.7 jit_solution(15970578605457710946)
XLA Ops:
  0.6 0.0 copy-start.7
  0.6 0.0 copy-start.4
  0.7 1.4 copy.19.pd_col_ref
  2.1 1.4 copy.20.ra_col_ref
  3.4 1.0 convert_element_type.9
  4.4 2.3 %pad_maximum_fusion.wd_ref = bf16[512,1152]{1,0:T(8,128)(2,1)} fusion(bf16[512,128]{1,0:T(8,128)(2,1)S(1)} %convert_element_type.9, bf16[512,1024]{1,0:T(8,128)(2,1)} %param.14), kind=kLoop, calls=%fused_computation | loop fusion | flops 2359296 | bytes 2359296 | tf_op jit(solution)/shard_map/concatenate | solution.py:449
  6.7 0.0 copy-done.4
  6.8 0.0 copy-done.7
  6.8 0.6 maximum_maximum_fusion.upad_ref
  7.4 0.0 copy-start.1
  7.4 0.0 copy-start.2
  7.4 0.0 copy-start.3
  7.4 0.0 copy-start.5
  7.4 0.0 copy-start.6
  7.4 133.8 %shard_map.170 = (bf16[128,1024]{1,0:T(8,128)(2,1)}, bf16[128,8192]{1,0:T(8,128)(2,1)}, f32[512,128]{1,0:T(8,128)}, f32[16,512]{1,0:T(8,128)}) custom-call(bf16[128,8192]{1,0:T(8,128)(2,1)} %x_ref.1, s32[128,1]{1,0:T(8,128)} %copy.19.pd_col_ref, s32[1,128]{1,0:T(1,128)} %bitcast.5, s32[128,1]{1,0:T(8,128)} %copy.20.ra_col_ref, ...), custom_call_target="tpu_custom_call" | custom-call | flops 7247757312 | bytes 23068672 | tf_op jit(solution)/shard_map/pallas_call | solution.py:458
  141.2 0.0 copy-start
  141.2 0.0 copy-done.1
  141.3 0.0 copy-done.2
  141.3 0.0 copy-done.3
  141.3 2.1 %divide_subtract_fusion = (f32[512,128]{1,0:T(8,128)}, f32[512,128]{1,0:T(8,128)}, f32[512,128]{1,0:T(8,128)}) fusion(f32[512,128]{1,0:T(8,128)S(1)} %copy-done.1, f32[512,128]{1,0:T(8,128)} %get-tuple-element.14, f32[512,128]{1,0:T(8,128)S(1)} %copy-done.2, f32[512,128]{1,0:T(8,128)S(1)} %copy-done.3), kind=kLoop, calls=%fused_computation.3 | loop fusion | flops 786432 | bytes 1835008 | tf_op jit(solution)/shard_map/sub | solution.py:29
  143.3 0.7 fusion.4
  144.1 0.0 copy-done.5
  144.1 0.0 copy-done.6
  144.1 0.7 divide_subtract_fusion.1
  144.7 1.7 %copy.23 = bf16[128,1024]{1,0:T(8,128)(2,1)} copy(bf16[128,1024]{1,0:T(8,128)(2,1)} %get-tuple-element.34) | data formatting | bytes 524288
  146.4 0.0 copy-done
  146.4 1.3 copy.24
  (4 shorter events, 0.0 us)
Async XLA Ops:
  0.6 6.1 %copy-start.7 = (s32[128]{0:T(128)S(1)}, s32[128]{0:T(128)}, u32[]{:S(2)}) copy-start(s32[128]{0:T(128)} %param.13) | copy-start | bytes 1540
  0.6 6.1 %copy-start.4 = (f32[8,1024]{1,0:T(8,128)S(1)}, f32[8,1024]{1,0:T(8,128)}, u32[]{:S(2)}) copy-start(f32[8,1024]{1,0:T(8,128)} %param.16) | copy-start | bytes 98308
  7.4 133.8 %copy-start.1 = (f32[512,128]{1,0:T(8,128)S(1)}, f32[512,128]{1,0:T(8,128)}, u32[]{:S(2)}) copy-start(f32[512,128]{1,0:T(8,128)} %param.15) | copy-start | bytes 786436
  7.4 133.8 %copy-start.2 = (f32[512,128]{1,0:T(8,128)S(1)}, f32[512,128]{1,0:T(8,128)}, u32[]{:S(2)}) copy-start(f32[512,128]{1,0:T(8,128)} %param.17) | copy-start | bytes 786436
  7.4 133.9 %copy-start.3 = (f32[512,128]{1,0:T(8,128)S(1)}, f32[512,128]{1,0:T(8,128)}, u32[]{:S(2)}) copy-start(f32[512,128]{1,0:T(8,128)} %param.18) | copy-start | bytes 786436
  7.4 136.7 %copy-start.5 = (f32[8,1024]{1,0:T(8,128)S(1)}, f32[8,1024]{1,0:T(8,128)}, u32[]{:S(2)}) copy-start(f32[8,1024]{1,0:T(8,128)} %param.19) | copy-start | bytes 98308
  7.4 136.7 %copy-start.6 = (f32[8,1024]{1,0:T(8,128)S(1)}, f32[8,1024]{1,0:T(8,128)}, u32[]{:S(2)}) copy-start(f32[8,1024]{1,0:T(8,128)} %param.20) | copy-start | bytes 98308
  141.2 5.2 %copy-start = (bf16[128,8192]{1,0:T(8,128)(2,1)S(1)}, bf16[128,8192]{1,0:T(8,128)(2,1)}, u32[]{:S(2)}) copy-start(bf16[128,8192]{1,0:T(8,128)(2,1)} %get-tuple-element.35) | copy-start | bytes 6291460
